TPU v7x, 32 devices: a whole 2x2x4 slice. The times are simulated.
32 devices in a mesh: slides: 1, row: 2 (over core), col: 16 (over z, y, x).
Axes of the slice: x: 2, y: 2, z: 4, core: 2. Of those that a mesh axis runs over, the one named last changes fastest.
Arguments:
- slide: bfloat16 [56, 112, 1024], P(('slides', 'row'), 'col'), may hold values from -6 to 6
- tissue: int32 [56, 112], P(('slides', 'row'), 'col'), may hold values from 0 to 1, as said below
- w_in: bfloat16 [1024, 2048], replicated, may hold values from -0.1875 to 0.1875
- w_bcd: bfloat16 [1024, 48], replicated, may hold values from -0.1875 to 0.1875
- dt_bias: float32 [16], replicated, may hold values from -2 to 1
- rate_x: float32 [16], replicated, as said below
- rate_y: float32 [16], replicated, as said below
- d_skip: float32 [16], replicated, may hold values from 0.5 to 2
- norm_gain: float32 [1024], replicated, may hold values from 0.1 to 1.9
- w_out: bfloat16 [1024, 1024], replicated, may hold values from -0.1875 to 0.1875
Outputs:
- mixed: bfloat16 [56, 112, 1024], P(('slides', 'row'), 'col')
Inputs may be any that keep to these rules, and one draw needn't show every extreme that they name: 1 marks a tissue patch, 0 background. `rate_x`: positive decay rates per head. `rate_y`: positive decay rates per head.
All inputs are finite; a program needn't handle non-finite values.
Results may differ from a plain program's by a relative error of at most 0.013.
Values may be sent and summed in bfloat16 or wider, within the bound.
A program may use at most 320 MiB of HBM per device.

v0:
```python
import jax
import jax.numpy as jnp
from jax import lax
from jax.sharding import PartitionSpec as P

norm_eps = 1e-05


def carried_in_2(value, axis, join, neutral):
    count, mine = (lax.axis_size(axis), lax.axis_index(axis))
    pieces = jax.tree.map(lambda part: lax.all_gather(part, axis), value)
    so_far = jax.tree.map(
        lambda part, zero: jnp.full_like(part, 0) + jnp.asarray(zero, part.dtype), value, neutral
    )

    def hop(position, so_far):
        longer = join(so_far, jax.tree.map(lambda part: part[position], pieces))
        return jax.tree.map(lambda new, old: jnp.where(position < mine, new, old), longer, so_far)

    return lax.fori_loop(0, count - 1, hop, so_far)


def chain_join(earlier, later):
    return (earlier[0] + later[0], jnp.exp(later[0]) * earlier[1] + later[1])


def per_device(slide, tissue, w_in, w_bcd, dt_bias, rate_x, rate_y, d_skip, norm_gain, w_out):
    tile_rows, tile_cols, model_width = slide.shape
    inner_width = w_out.shape[0]
    head_count = dt_bias.shape[0]
    head_width = inner_width // head_count
    state_size = (w_bcd.shape[1] - head_count) // 2
    cell_mask = tissue.astype(jnp.float32).reshape(tile_rows * tile_cols, 1)
    flat_cells = slide.reshape(tile_rows * tile_cols, model_width)
    has_tissue = jnp.any(tissue > 0)

    def project_cells():
        projected = jnp.dot(flat_cells, w_in, preferred_element_type=jnp.float32)
        values = projected[:, :inner_width].astype(jnp.bfloat16) * cell_mask.astype(jnp.bfloat16)
        gate_part = projected[:, inner_width:].astype(jnp.bfloat16)
        terms = jnp.dot(flat_cells, w_bcd, preferred_element_type=jnp.float32)
        step_part = (cell_mask * jax.nn.softplus(terms[:, 2 * state_size :] + dt_bias)).astype(
            jnp.bfloat16
        )
        packed = jnp.concatenate(
            [terms[:, : 2 * state_size].astype(jnp.bfloat16), step_part], axis=1
        )
        return (values, gate_part, packed)

    def empty_terms():
        return (
            jnp.zeros((tile_rows * tile_cols, inner_width), jnp.bfloat16),
            jnp.zeros((tile_rows * tile_cols, inner_width), jnp.bfloat16),
            jnp.zeros((tile_rows * tile_cols, 2 * state_size + head_count), jnp.bfloat16),
        )

    values, gate_z, packed = lax.cond(has_tissue, project_cells, empty_terms)
    step_cells = (
        packed[:, 2 * state_size :].astype(jnp.float32).reshape(tile_rows, tile_cols, head_count)
    )
    b_cells = packed[:, :state_size].astype(jnp.float32).reshape(tile_rows, tile_cols, state_size)
    c_cells = (
        packed[:, state_size : 2 * state_size]
        .astype(jnp.float32)
        .reshape(tile_rows, tile_cols, state_size)
    )
    vals_cells = values.astype(jnp.float32).reshape(tile_rows, tile_cols, inner_width)
    step_chan = jnp.repeat(step_cells, head_width, axis=2)
    source_cells = step_chan * vals_cells
    log_x = -step_chan * jnp.repeat(rate_x, head_width)
    decay_x = jnp.exp(log_x)
    log_y = -step_chan * jnp.repeat(rate_y, head_width)
    decay_y = jnp.exp(log_y)
    edge = jnp.zeros((tile_rows, state_size, inner_width), jnp.float32)
    for column in range(tile_cols):
        edge = (
            decay_x[:, column, None, :] * edge
            + b_cells[:, column, :, None] * source_cells[:, column, None, :]
        )
    log_edge = jnp.sum(log_x, axis=1)[:, None, :]
    from_left = carried_in_2(
        (log_edge, edge), "col", chain_join, (jnp.zeros_like(log_edge), jnp.zeros_like(edge))
    )
    entry_left = from_left[1]

    def cell_row(carry, row_data):
        vertical, cum = carry
        a_row, ay_row, ly_row, u_row, b_row, c_row, left = row_data
        running = left
        pieces = []
        for column in range(tile_cols):
            running = (
                a_row[column][None, :] * running + b_row[column][:, None] * u_row[column][None, :]
            )
            pieces.append(running)
        vertical = ay_row[:, None, :] * vertical + jnp.stack(pieces)
        cum = cum + ly_row[:, None, :]
        out_row = jnp.einsum("jn,jnc->jc", c_row, vertical, precision=lax.Precision.HIGHEST)
        return ((vertical, cum), (out_row, cum[:, 0, :]))

    start = (
        jnp.zeros((tile_cols, state_size, inner_width), jnp.float32),
        jnp.zeros((tile_cols, 1, inner_width), jnp.float32),
    )
    (bottom_state, bottom_log), (local_out, cum_rows) = lax.scan(
        cell_row, start, (decay_x, decay_y, log_y, source_cells, b_cells, c_cells, entry_left)
    )
    top_zero = (jnp.zeros_like(bottom_log), jnp.zeros_like(bottom_state))
    from_above = carried_in_2((bottom_log, bottom_state), "row", chain_join, top_zero)
    entry_down = from_above[1]
    carried_in = jnp.einsum("ijn,jnc->ijc", c_cells, entry_down, precision=lax.Precision.HIGHEST)
    cell_out = (
        local_out + jnp.exp(cum_rows) * carried_in + jnp.repeat(d_skip, head_width) * vals_cells
    )
    y_cells = cell_out.astype(jnp.bfloat16).reshape(tile_rows * tile_cols, inner_width)

    def finish_cells():
        gated = y_cells.astype(jnp.float32) * jax.nn.silu(gate_z.astype(jnp.float32))
        scaled = (
            gated
            * lax.rsqrt(jnp.mean(gated * gated, axis=-1, keepdims=True) + norm_eps)
            * norm_gain
        )
        result = (
            jnp.dot(scaled.astype(jnp.bfloat16), w_out, preferred_element_type=jnp.float32)
            * cell_mask
        )
        return result.astype(jnp.bfloat16)

    def empty_output():
        return jnp.zeros((tile_rows * tile_cols, model_width), jnp.bfloat16)

    final_cells = lax.cond(has_tissue, finish_cells, empty_output)
    return final_cells.reshape(tile_rows, tile_cols, model_width)


def solution(mesh):
    placed = (
        P(("slides", "row"), "col", None),
        P(("slides", "row"), "col"),
        P(),
        P(),
        P(),
        P(),
        P(),
        P(),
        P(),
        P(),
    )
    return jax.shard_map(
        per_device,
        mesh=mesh,
        in_specs=placed,
        out_specs=P(("slides", "row"), "col", None),
        check_vma=False,
    )
```

profile of v0, /device:TPU:1, one launch (start us, length us, event | category | flops | bytes accessed | tf_op | source)
XLA Modules:
  0.0 691.2 jit_solution(13298296646756493034)
XLA Ops:
  9.4 7.1 %conditional.2 = (bf16[196,1024]{1,0:T(8,128)(2,1)S(1)}, bf16[196,48]{0,1:T(8,128)(2,1)S(1)}, f32[28,7,1024]{2,0,1:T(8,128)S(1)}) conditional(s32[]{:T(128)} %convert_element_type.41, () %tuple.44, (bf16[28,7,1024]{2,1,0:T(8,128)(2,1)}, bf16[1024,2048]{1,0:T(8,128)(2,1)}, bf16[1024,48]{0,1:T(8,128)(2,1)}, f32[196,1]{0,1:T(1,128)S(1)}, ...), branch_computations={%region_1.0_spmd, %region_2.3_spmd} | conditional | flops 842220032 | bytes 12040968 | solution.py:57
  12.5 3.2 convolution_convert_fusion
  19.6 2.1 fusion.36
  23.4 2.8 multiply_add_fusion.6
  27.0 51.2 %all-gather.5.cloned.1.call-done = f32[16,28,1,1024]{3,2,1,0:T(1,128)} async-done(((f32[1,28,1,1024]{3,2,1,0:T(1,128)}), f32[16,28,1,1024]{3,2,1,0:T(1,128)}) %all-gather.5.cloned.1.call-update) | async-done | bytes 1835024 | tf_op jit(solution)/shard_map/all_gather | solution.py:11
  78.2 313.5 %all-gather.7.cloned.1.call-done = f32[16,28,16,1024]{3,2,1,0:T(8,128)} async-done(((f32[1,28,16,1024]{3,2,1,0:T(8,128)}), f32[16,28,16,1024]{3,2,1,0:T(8,128)}) %all-gather.7.cloned.1.call-update) | async-done | bytes 29360144 | tf_op jit(solution)/shard_map/all_gather | solution.py:11
  391.8 60.2 %while.36 = (s32[]{:T(128)}, f32[28,16,1024]{2,1,0:T(8,128)S(1)}, s32[]{:T(128)}, f32[16,28,1,1024]{3,2,1,0:T(1,128)}, f32[16,28,16,1024]{3,2,1,0:T(8,128)}, /*index=5*/s32[]{:T(128)}, s32[]{:T(128)}) while((s32[]{:T(128)}, f32[28,16,1024]{2,1,0:T(8,128)S(1)}, s32[]{:T(128)}, f32[16,28,1,1024]{3,2,1,0:T(1,128)}, ...), condition=%wide.region_5.6_spmd.clone, body=%wide.region_4.5_spmd.clone.sunk | while | flops 1835012 | bytes 6078569 | solution.py:20
  392.7 3.0 fusion.58
  396.8 3.0 fusion.58
  400.8 3.0 fusion.58
  404.8 3.0 fusion.58
  408.8 3.0 fusion.58
  412.8 3.0 fusion.58
  416.8 3.0 fusion.58
  420.8 3.0 fusion.58
  424.8 3.0 fusion.58
  428.9 3.0 fusion.58
  432.9 3.0 fusion.58
  436.9 3.0 fusion.58
  440.9 3.0 fusion.58
  444.9 3.0 fusion.58
  448.9 3.0 fusion.58
  452.0 220.8 %while.37 = (s32[]{:T(128)}, f32[7,16,1024]{2,1,0:T(8,128)S(1)}, f32[7,1,1024]{2,1,0:T(1,128)S(1)}, f32[28,7,1024]{2,0,1:T(8,128)}, f32[28,7,1024]{2,0,1:T(8,128...) while((s32[]{:T(128)}, f32[7,16,1024]{2,1,0:T(8,128)S(1)}, ...), condition=%wide.region_7.8_spmd.clone, body=%wide.region_6.7_spmd.clone.sunk | while | flops 3110920 | bytes 3601364 | solution.py:105
  455.4 1.8 dynamic_update_slice.11
  463.3 1.8 dynamic_update_slice.11
  471.2 1.8 dynamic_update_slice.11
  479.1 1.8 dynamic_update_slice.11
  487.0 1.8 dynamic_update_slice.11
  494.9 1.8 dynamic_update_slice.11
  502.7 1.8 dynamic_update_slice.11
  510.6 1.8 dynamic_update_slice.11
  518.5 1.8 dynamic_update_slice.11
  526.4 1.8 dynamic_update_slice.11
  534.3 1.8 dynamic_update_slice.11
  542.2 1.8 dynamic_update_slice.11
  550.1 1.8 dynamic_update_slice.11
  558.0 1.8 dynamic_update_slice.11
  565.9 1.8 dynamic_update_slice.11
  573.8 1.8 dynamic_update_slice.11
  647.4 1.8 dynamic_update_slice.12
  655.3 1.8 dynamic_update_slice.12
  663.2 1.8 dynamic_update_slice.12
  671.1 1.8 dynamic_update_slice.12
  672.8 3.3 all-gather.1
  676.1 1.9 all-gather
  678.1 2.2 fusion.25
  680.3 3.3 conditional.3
  681.0 2.4 fusion
  (615 shorter events, 210.3 us)
Async XLA Ops:
  6.5 71.7 %all-gather.5.cloned.1.call-start = ((), (), s32[]{:S(2)}) async-start(), calls=%async_computation | async-start | bytes 1949696 | tf_op jit(solution)/shard_map/all_gather | solution.py:11
  9.4 7.3 %copy-start.5 = (f32[16]{0:T(128)S(1)}, f32[16]{0:T(128)}, u32[]{:S(2)}) copy-start(f32[16]{0:T(128)} %param.23) | copy-start | bytes 196
  16.5 1.6 copy-start.2
  16.5 3.1 copy-start
  18.0 373.8 %all-gather.7.cloned.1.call-start = ((), (), s32[]{:S(2)}) async-start(), calls=%async_computation.1 | async-start | bytes 31195136 | tf_op jit(solution)/shard_map/all_gather | solution.py:11
  18.1 1.0 copy-start.6
  26.2 0.7 copy-start.7
  672.8 5.2 copy-start.1
  678.0 2.2 copy-start.3
  678.0 2.2 copy-start.8
  683.6 0.8 copy-start.4
Sparse Core Ops, SparseCore 0:
  18.1 60.0 all-gather.4
  80.9 310.8 all-gather.6
where the time goes:
time: 698 us; the launch traced here: 691 us
  waiting for transfers between devices  365 us (52%)
  local copies, waits for them, and re-layouts  175 us (25%)
  other arithmetic  110 us (16%)
  matrix products  18.7 us (3%)
  between operations  14.4 us (2%)
    all_gather x2, waiting for transfers between devices, carried_in_2(): pieces = jax.tree.map(lambda part: lax.all_gather(part, axis), value)  365 us
    dynamic_update_slice x84, local copies, waits for them, and re-layouts, per_device(): lax.scan(cell_row, start, (decay_x, decay_y, log_y, source_cells, b_cells...  98.8 us
    select_n x15, other arithmetic, hop(): jnp.where(position < mine, new, old)  45.6 us
    slice x28, local copies, waits for them, and re-layouts, cell_row(): u_row[column][None, :]  28.3 us
    dynamic_slice x84, local copies, waits for them, and re-layouts, per_device(): lax.scan(cell_row, start, (decay_x, decay_y, log_y, source_cells, b_cells...  27.7 us
    add x28, other arithmetic, cell_row(): cum = cum + ly_row[:, None, :]  27.5 us
    while x168, other arithmetic  16.3 us
  transfers between devices with their start and end apart: 2, of which 2 were waited for; matrix products, arithmetic and copies ran while one was open for 1% of the time, Pallas kernels for 0%

commit v1 on v0

v1 whole, which is shorter than its diff:
```python
import functools

import jax
import jax.numpy as jnp
from jax import lax
from jax.experimental import pallas as pl
from jax.experimental.pallas import tpu as pltpu
from jax.sharding import PartitionSpec as P

norm_eps = 1e-05
LANES = 128
SUB = 8
MESH = pl.DeviceIdType.MESH
f32, bf16 = jnp.float32, jnp.bfloat16


def kernel(dims, slide_ref, mask_ref, wbcd_ref, bias_ref, gain_ref, ratex_ref, ratey_ref, skip_ref,
           win_hbm, wout_hbm, out_ref,
           win, wout, send, recv, zs, tsc, lsc, ysc, state, carry, ysend, yrecv, yfull,
           w_sem, s_sem, r_sem, ys_sem, yr_sem, cs_sem, cr_sem, l_sem):
    n_row, n_col, rows, cols, inner, heads, width, n_state, block = dims
    ch = inner // n_col
    jp = n_col * SUB
    cells = rows * SUB
    blocks = ch // block
    me = lax.axis_index("col")
    my_row = lax.axis_index("row")
    head = lax.div(me * ch, width)
    dt_at = ch + 2 * n_state

    w1 = pltpu.make_async_copy(win_hbm.at[:, pl.ds(0, inner)], win.at[:, pl.ds(0, inner)], w_sem.at[0])
    w2 = pltpu.make_async_copy(win_hbm.at[:, pl.ds(inner, inner)], win.at[:, pl.ds(inner, inner)], w_sem.at[1])
    w3 = pltpu.make_async_copy(wout_hbm, wout, w_sem.at[2])
    w1.start()
    w2.start()
    w3.start()

    barrier = pltpu.get_barrier_semaphore()
    for o in range(1, n_col):
        pl.semaphore_signal(barrier, inc=1, device_id={"col": lax.rem(me + o, n_col)}, device_id_type=MESH)

    @pl.when(my_row > 0)
    def _():
        pl.semaphore_signal(barrier, inc=1, device_id={"row": my_row - 1}, device_id_type=MESH)

    @pl.when(my_row < n_row - 1)
    def _():
        pl.semaphore_signal(barrier, inc=1, device_id={"row": my_row + 1}, device_id_type=MESH)

    x = slide_ref[...]
    mask = mask_ref[...]
    lane = lax.broadcasted_iota(jnp.int32, (cells, LANES), 1)
    terms = jnp.dot(x, wbcd_ref[...], preferred_element_type=f32)
    biased = terms + bias_ref[...]
    steps = mask * (jnp.maximum(biased, 0.0) + jnp.log1p(jnp.exp(-jnp.abs(biased))))
    w1.wait()
    per = LANES // ch
    for t in range(inner // LANES):
        vals = jnp.dot(x, win[:, t * LANES:(t + 1) * LANES], preferred_element_type=f32)
        vals = vals.astype(bf16).astype(f32) * mask
        for q in range(per):
            d = t * per + q
            h = (d * ch) // width
            moved = vals if q == 0 else pltpu.roll(vals, LANES - q * ch, 1)
            dts = steps if h == 0 else pltpu.roll(steps, LANES - h, 1)
            chunk = jnp.where(lane < ch, moved, jnp.where(lane < dt_at, terms, dts))
            send[d] = chunk.astype(bf16)

    beside = jnp.where(my_row > 0, 1, 0) + jnp.where(my_row < n_row - 1, 1, 0)
    pl.semaphore_wait(barrier, n_col - 1 + beside)

    def forth(o):
        return pltpu.make_async_remote_copy(
            src_ref=send.at[lax.rem(me + o, n_col)], dst_ref=recv.at[me],
            send_sem=s_sem.at[o], recv_sem=r_sem.at[o],
            device_id={"col": lax.rem(me + o, n_col)}, device_id_type=MESH)

    for o in range(1, n_col):
        forth(o).start()
    own = pltpu.make_async_copy(send.at[me], recv.at[me], l_sem.at[0])
    own.start()

    w2.wait()
    for t in range(inner // LANES):
        zs[:, t * LANES:(t + 1) * LANES] = jnp.dot(
            x, win[:, inner + t * LANES:inner + (t + 1) * LANES], preferred_element_type=f32).astype(bf16)

    own.wait()
    for o in range(1, n_col):
        pltpu.make_async_remote_copy(
            src_ref=send.at[lax.rem(me + o, n_col)], dst_ref=recv.at[lax.rem(me + n_col - o, n_col)],
            send_sem=s_sem.at[o], recv_sem=r_sem.at[o],
            device_id={"col": lax.rem(me + o, n_col)}, device_id_type=MESH).wait()

    rate_x, rate_y, skip = ratex_ref[head], ratey_ref[head], skip_ref[head]
    down = lax.broadcasted_iota(jnp.int32, (jp, jp), 0)
    along = lax.broadcasted_iota(jnp.int32, (jp, jp), 1)
    tri = (along <= down).astype(bf16)
    cell_lane = lax.broadcasted_iota(jnp.int32, (jp, LANES), 1)

    def prepare(k, _):
        both = recv[:, pl.ds(pl.multiple_of(k * 16, 16), 16), :].astype(f32)
        for p in range(2):
            here = both[:, p * SUB:(p + 1) * SUB, :].reshape(jp, LANES)
            sums = jnp.dot(tri, here.astype(bf16), preferred_element_type=f32)
            sum_col = sums[:, dt_at:dt_at + 1]
            turned = jnp.where(cell_lane == dt_at + 1, sum_col, here).T
            tsc[2 * k + p] = turned
            gap = turned[dt_at + 1:dt_at + 2, :] - sum_col
            lsc[2 * k + p] = jnp.exp(jnp.where(down <= along, -rate_x * gap, -1e30)).astype(bf16)
        return 0

    lax.fori_loop(0, rows // 2, prepare, 0)

    def pass_down(cb):
        return pltpu.make_async_remote_copy(
            src_ref=state.at[cb], dst_ref=carry.at[cb],
            send_sem=cs_sem.at[cb], recv_sem=cr_sem.at[cb],
            device_id={"row": my_row + 1}, device_id_type=MESH)

    for cb in range(blocks):
        @pl.when(my_row == 0)
        def _():
            state[cb] = jnp.zeros_like(state[cb])

        @pl.when(my_row > 0)
        def _():
            pltpu.make_async_remote_copy(
                src_ref=state.at[cb], dst_ref=carry.at[cb],
                send_sem=cs_sem.at[cb], recv_sem=cr_sem.at[cb],
                device_id={"row": my_row - 1}, device_id_type=MESH).wait_recv()
            state[cb] = carry[cb]

        def one_row(i, _):
            v = tsc[i, cb * block:(cb + 1) * block, :]
            b = tsc[i, ch:ch + n_state, :]
            c = tsc[i, ch + n_state:ch + 2 * n_state, :]
            dt = tsc[i, dt_at:dt_at + 1, :]
            source = (b[:, None, :] * (v * dt)[None, :, :]).reshape(n_state * block, jp)
            hx = jnp.dot(source.astype(bf16), lsc[i], preferred_element_type=f32)
            now = jnp.exp(-rate_y * dt) * state[cb] + hx
            state[cb] = now
            y = jnp.sum(c[:, None, :] * now.reshape(n_state, block, jp), axis=0) + skip * v
            ysc[i, cb * block:(cb + 1) * block, :] = y
            return 0

        lax.fori_loop(0, rows, one_row, 0)

        @pl.when(my_row < n_row - 1)
        def _():
            pass_down(cb).start()

    def give_back(m, _):
        parts = []
        for g in range(2):
            pair = [ysc[4 * m + 2 * g], ysc[4 * m + 2 * g + 1]]
            if 2 * ch < LANES:
                pair.append(jnp.zeros((LANES - 2 * ch, jp), f32))
            parts.append(jnp.concatenate(pair, axis=0).T.reshape(n_col, SUB, LANES))
        ysend[:, pl.ds(pl.multiple_of(m * 16, 16), 16), :] = jnp.concatenate(parts, axis=1).astype(bf16)
        return 0

    lax.fori_loop(0, rows // 4, give_back, 0)

    def back(o):
        return pltpu.make_async_remote_copy(
            src_ref=ysend.at[lax.rem(me + o, n_col)], dst_ref=yrecv.at[me],
            send_sem=ys_sem.at[o], recv_sem=yr_sem.at[o],
            device_id={"col": lax.rem(me + o, n_col)}, device_id_type=MESH)

    for o in range(1, n_col):
        back(o).start()
    own_y = pltpu.make_async_copy(ysend.at[me], yrecv.at[me], l_sem.at[1])
    own_y.start()

    @pl.when(my_row < n_row - 1)
    def _():
        for cb in range(blocks):
            pass_down(cb).wait_send()

    w3.wait()
    own_y.wait()
    for o in range(1, n_col):
        pltpu.make_async_remote_copy(
            src_ref=ysend.at[lax.rem(me + o, n_col)], dst_ref=yrecv.at[lax.rem(me + n_col - o, n_col)],
            send_sem=ys_sem.at[o], recv_sem=yr_sem.at[o],
            device_id={"col": lax.rem(me + o, n_col)}, device_id_type=MESH).wait()

    half_lane = lax.broadcasted_iota(jnp.int32, (cells // 2, LANES), 1)
    squares = jnp.zeros((cells, 1), f32)
    for t in range(inner // LANES):
        parts = []
        for p in range(2):
            tile = None
            for q in range(per):
                piece = yrecv[t * per + q].astype(f32)
                shift = ((q - p) * ch) % LANES
                if shift:
                    piece = pltpu.roll(piece, shift, 1)
                tile = piece if tile is None else jnp.where(half_lane < q * ch, tile, piece)
            parts.append(tile.reshape(rows // 2, 1, SUB, LANES))
        y = jnp.concatenate(parts, axis=1).reshape(cells, LANES)
        z = zs[:, t * LANES:(t + 1) * LANES].astype(f32)
        g = y * (z * jax.nn.sigmoid(z))
        squares = squares + jnp.sum(g * g, axis=1, keepdims=True)
        yfull[:, t * LANES:(t + 1) * LANES] = g
    scale = lax.rsqrt(squares / inner + norm_eps)
    normed = (yfull[...] * scale * gain_ref[...]).astype(bf16)
    mixed = jnp.dot(normed, wout[...], preferred_element_type=f32) * mask
    out_ref[...] = mixed.reshape(rows, SUB, mixed.shape[1])[:, :cols, :].astype(bf16)


def per_device(slide, tissue, w_in, w_bcd, dt_bias, rate_x, rate_y, d_skip, norm_gain, w_out):
    rows, cols, model = slide.shape
    inner, heads = w_out.shape[0], dt_bias.shape[0]
    n_state = (w_bcd.shape[1] - heads) // 2
    width = inner // heads
    n_col, n_row = lax.axis_size("col"), lax.axis_size("row")
    ch = inner // n_col
    block = min(ch, 16)
    jp, cells = n_col * SUB, rows * SUB
    assert cols <= SUB and rows % 4 == 0 and 2 * ch <= LANES and width % ch == 0
    assert ch + 2 * n_state + heads <= LANES and ch % block == 0
    pad = SUB - cols
    x = jnp.pad(slide, ((0, 0), (0, pad), (0, 0))).reshape(cells, model)
    mask = jnp.pad(tissue.astype(f32), ((0, 0), (0, pad))).reshape(cells, 1)
    room = LANES - ch - w_bcd.shape[1]
    wbcd = jnp.pad(w_bcd, ((0, 0), (ch, room)))
    bias = jnp.pad(dt_bias, (ch + 2 * n_state, room)).reshape(1, LANES)
    vmem = pl.BlockSpec(memory_space=pltpu.VMEM)
    smem = pl.BlockSpec(memory_space=pltpu.SMEM)
    hbm = pl.BlockSpec(memory_space=pl.ANY)
    blocks = ch // block
    dims = (n_row, n_col, rows, cols, inner, heads, width, n_state, block)
    dma = pltpu.SemaphoreType.DMA
    return pl.pallas_call(
        functools.partial(kernel, dims),
        out_shape=jax.ShapeDtypeStruct((rows, cols, model), bf16),
        in_specs=[vmem] * 5 + [smem] * 3 + [hbm] * 2,
        out_specs=vmem,
        scratch_shapes=[
            pltpu.VMEM(w_in.shape, bf16),
            pltpu.VMEM(w_out.shape, bf16),
            pltpu.VMEM((n_col, cells, LANES), bf16),
            pltpu.VMEM((n_col, cells, LANES), bf16),
            pltpu.VMEM((cells, inner), bf16),
            pltpu.VMEM((rows, LANES, jp), f32),
            pltpu.VMEM((rows, jp, jp), bf16),
            pltpu.VMEM((rows, ch, jp), f32),
            pltpu.VMEM((blocks, n_state * block, jp), f32),
            pltpu.VMEM((blocks, n_state * block, jp), f32),
            pltpu.VMEM((n_col, cells // 2, LANES), bf16),
            pltpu.VMEM((n_col, cells // 2, LANES), bf16),
            pltpu.VMEM((cells, inner), f32),
            dma((3,)), dma((n_col,)), dma((n_col,)), dma((n_col,)), dma((n_col,)),
            dma((blocks,)), dma((blocks,)), dma((2,)),
        ],
        compiler_params=pltpu.CompilerParams(
            collective_id=0, has_side_effects=True, vmem_limit_bytes=60 * 1024 * 1024),
        cost_estimate=pl.CostEstimate(flops=4 * 10**9, bytes_accessed=8 * 10**6, transcendentals=10**6),
    )(x, mask, wbcd, bias, norm_gain.reshape(1, inner), rate_x, rate_y, d_skip, w_in, w_out)


def solution(mesh):
    grid = P(("slides", "row"), "col")
    return jax.shard_map(
        per_device,
        mesh=mesh,
        in_specs=(P(("slides", "row"), "col", None), grid) + (P(),) * 8,
        out_specs=P(("slides", "row"), "col", None),
        check_vma=False,
    )
```

time: 698 us -> 74.5 us (0.11)
  waiting for transfers between devices: 365 us -> 0 us
  local copies, waits for them, and re-layouts: 175 us -> 7.74 us
  other arithmetic: 110 us -> 0.69 us
  Pallas kernels: 0 us -> 65.8 us
  matrix products: 18.7 us -> 0 us
  between operations: 14.4 us -> 0.02 us
    all_gather x2 -> x0, waiting for transfers between devices: 365 us -> none  [carried_in_2(): pieces = jax.tree.map(lambda part: lax.all_gather(part, axis), value)]
    dynamic_update_slice x84 -> x0, local copies, waits for them, and re-layouts: 98.8 us -> none  [per_device(): lax.scan(cell_row, start, (decay_x, decay_y, log_y, source_cells, b_cells...]
    pallas_call x0 -> x1, Pallas kernels: none -> 65.8 us  [per_device(): pl.pallas_call(functools.partial(kernel, dims), out_shape=jax.ShapeDtypeS...]
    select_n x15 -> x0, other arithmetic: 45.6 us -> none  [hop(): jnp.where(position < mine, new, old)]
    dynamic_slice x99 -> x0, local copies, waits for them, and re-layouts: 41.3 us -> none  [the longest x84 27.7 us: per_device(): lax.scan(cell_row, start, (decay_x, decay_y, log_y, source_cells, b_cells...]
    add x57 -> x0, other arithmetic: 36.6 us -> none  [the longest x28 27.5 us: cell_row(): cum = cum + ly_row[:, None, :]]
    slice x31 -> x0, local copies, waits for them, and re-layouts: 28.5 us -> none  [the longest x28 28.3 us: cell_row(): u_row[column][None, :]]
    dot_general x32 -> x0, matrix products: 18.7 us -> none  [the longest x28 9.75 us: cell_row(): jnp.einsum('jn,jnc->jc', c_row, vertical, precision=lax.Precision.HIGHEST)]
  transfers between devices with their start and end apart: 2 -> 0, of which waited for: 2 -> 0; matrix products, arithmetic and copies ran while one was open for 1% -> 0% of each run, Pallas kernels for 0% -> 0%
where the time goes in v1:
time: 74.5 us; the launch traced here: 74.3 us
  Pallas kernels  65.8 us (88%)
  local copies, waits for them, and re-layouts  7.74 us (10%)
    pallas_call x1, Pallas kernels, per_device(): pl.pallas_call(functools.partial(kernel, dims), out_shape=jax.ShapeDtypeS...  65.8 us
    unnamed x3, local copies, waits for them, and re-layouts  2.98 us
    reshape x1, local copies, waits for them, and re-layouts, per_device(): x = jnp.pad(slide, ((0, 0), (0, pad), (0, 0))).reshape(cells, model)  1.88 us

profile of v1, /device:TPU:1, one launch (start us, length us, event | category | flops | bytes accessed | tf_op | source)
XLA Modules:
  0.0 74.3 jit_solution(5733962208242494198)
XLA Ops:
  0.0 1.3 %pad_bitcast_fusion.1.bias_ref = f32[1,128]{1,0:T(1,128)} fusion(f32[16]{0:T(128)} %param.14), kind=kLoop, calls=%fused_computation.1 | loop fusion | bytes 576 | tf_op jit(solution)/shard_map/reshape | solution.py:229
  1.3 0.7 convert_element_type.11
  2.0 0.1 copy.16
  2.1 0.7 reshape.16.mask_ref
  2.8 1.1 %copy.14 = bf16[1024,48]{1,0:T(8,128)(2,1)S(1)} copy(bf16[1024,48]{0,1:T(8,128)(2,1)} %param.13) | data formatting | bytes 196608 | tf_op args[3]
  3.9 0.8 %pad.18.wbcd_ref = bf16[1024,128]{1,0:T(8,128)(2,1)} pad(bf16[1024,48]{1,0:T(8,128)(2,1)S(1)} %copy.14, bf16[]{:T(256)} %constant.3.clone.1), padding=0_0x64_16 | pad | bytes 360450 | tf_op jit(solution)/shard_map/jit(_pad)/pad | solution.py:228
  4.7 1.9 %pad_bitcast_fusion.slide_ref = bf16[224,1024]{1,0:T(8,128)(2,1)} fusion(bf16[28,7,1024]{2,1,0:T(8,128)(2,1)} %param.10), kind=kLoop, calls=%fused_computation | loop fusion | bytes 860160 | tf_op jit(solution)/shard_map/reshape | solution.py:225
  6.6 65.8 %shard_map.100 = bf16[28,7,1024]{2,1,0:T(8,128)(2,1)} custom-call(bf16[224,1024]{1,0:T(8,128)(2,1)} %pad_bitcast_fusion.slide_ref, f32[224,1]{1,0:T(8,128)} %reshape.16.mask_ref, bf16[1024,128]{1,0:T(8,128)(2,1)} %pad.18.wbcd_ref, f32[1,128]{1,0:T(1,128)} %pad_bitcast_fusion.1.bias_ref, f32[1,1024]{1,0:T(1,128)} %bitcast.5, f32[16]{0:T(128)} %ratex_ref.1, ...), custom_call_target="tpu_custom_call" | custom-call | flops 4000000000 | bytes 8000000 | tf_op jit(solution)/shard_map/pallas_call | solution.py:236
  72.4 1.8 %copy.18 = bf16[28,7,1024]{2,1,0:T(8,128)(2,1)} copy(bf16[28,7,1024]{2,1,0:T(8,128)(2,1)} %shard_map.100) | data formatting | bytes 802816
  (1 shorter events, 0.0 us)

commit v2 on v1

v2 whole, which is shorter than its diff:
```python
import functools

import jax
import jax.numpy as jnp
from jax import lax
from jax.experimental import pallas as pl
from jax.experimental.pallas import tpu as pltpu
from jax.sharding import PartitionSpec as P

norm_eps = 1e-05
LANES = 128
SUB = 8
MESH = pl.DeviceIdType.MESH
f32, bf16 = jnp.float32, jnp.bfloat16


def kernel(dims, slide_ref, tissue_ref, wbcd_ref, gain_ref, bias_ref, ratex_ref, ratey_ref, skip_ref,
           win_hbm, wout_hbm, out_ref,
           win, wout, send, recv, zs, tsc, fade, ysc, state, carry, ysend, yrecv, yfull,
           w_sem, s_sem, r_sem, ys_sem, yr_sem, cs_sem, cr_sem, l_sem):
    n_row, n_col, rows, cols, inner, heads, width, n_state, block, groups = dims
    ch = inner // n_col
    jp = n_col * SUB
    cells = rows * SUB
    blocks = ch // block
    me = lax.axis_index("col")
    my_row = lax.axis_index("row")
    head = lax.div(me * ch, width)
    dt_at = ch + 2 * n_state

    w1 = pltpu.make_async_copy(win_hbm.at[:, pl.ds(0, inner)], win.at[:, pl.ds(0, inner)], w_sem.at[0])
    w2 = pltpu.make_async_copy(win_hbm.at[:, pl.ds(inner, inner)], win.at[:, pl.ds(inner, inner)], w_sem.at[1])
    w3 = pltpu.make_async_copy(wout_hbm, wout, w_sem.at[2])
    w1.start()
    w2.start()
    w3.start()

    barrier = pltpu.get_barrier_semaphore()
    for o in range(1, n_col):
        pl.semaphore_signal(barrier, inc=1, device_id={"col": lax.rem(me + o, n_col)}, device_id_type=MESH)

    @pl.when(my_row > 0)
    def _():
        pl.semaphore_signal(barrier, inc=1, device_id={"row": my_row - 1}, device_id_type=MESH)

    @pl.when(my_row < n_row - 1)
    def _():
        pl.semaphore_signal(barrier, inc=1, device_id={"row": my_row + 1}, device_id_type=MESH)

    gap = jnp.zeros((rows, SUB - cols, slide_ref.shape[2]), f32)
    x = jnp.concatenate([slide_ref[...].astype(f32), gap], axis=1).reshape(cells, -1).astype(bf16)
    marks = jnp.concatenate([tissue_ref[...].astype(f32), jnp.zeros((SUB - cols, rows), f32)], axis=0)
    marks = jnp.concatenate([marks, jnp.zeros((SUB, LANES - rows), f32)], axis=1).T[:rows, :]
    spread = jnp.broadcast_to(marks[:, None, :], (rows, SUB, SUB))
    same = (lax.broadcasted_iota(jnp.int32, (rows, SUB, SUB), 1)
            == lax.broadcasted_iota(jnp.int32, (rows, SUB, SUB), 2))
    mask = jnp.sum(jnp.where(same, spread, 0.0), axis=2, keepdims=True).reshape(cells, 1)
    lane = lax.broadcasted_iota(jnp.int32, (cells, LANES), 1)
    terms = lax.dot_general(x, wbcd_ref[...], (((1,), (1,)), ((), ())), preferred_element_type=f32)
    terms = jnp.concatenate(
        [jnp.zeros((cells, ch), f32), terms, jnp.zeros((cells, LANES - dt_at - heads), f32)], axis=1)
    bias_lane = lax.broadcasted_iota(jnp.int32, (1, LANES), 1)
    bias = jnp.zeros((1, LANES), f32)
    for h in range(heads):
        bias = jnp.where(bias_lane == dt_at + h, bias_ref[h], bias)
    biased = terms + bias
    steps = mask * (jnp.maximum(biased, 0.0) + jnp.log1p(jnp.exp(-jnp.abs(biased))))
    w1.wait()
    per = LANES // ch
    for t in range(inner // LANES):
        vals = jnp.dot(x, win[:, t * LANES:(t + 1) * LANES], preferred_element_type=f32)
        vals = vals.astype(bf16).astype(f32) * mask
        for q in range(per):
            d = t * per + q
            h = (d * ch) // width
            moved = vals if q == 0 else pltpu.roll(vals, LANES - q * ch, 1)
            dts = steps if h == 0 else pltpu.roll(steps, LANES - h, 1)
            chunk = jnp.where(lane < ch, moved, jnp.where(lane < dt_at, terms, dts))
            send[d] = chunk.astype(bf16)

    beside = jnp.where(my_row > 0, 1, 0) + jnp.where(my_row < n_row - 1, 1, 0)
    pl.semaphore_wait(barrier, n_col - 1 + beside)

    def forth(g, o, landing):
        start, size = groups[g]
        part = pl.ds(start * SUB, size * SUB)
        return pltpu.make_async_remote_copy(
            src_ref=send.at[lax.rem(me + o, n_col), part], dst_ref=recv.at[landing, part],
            send_sem=s_sem.at[g, o], recv_sem=r_sem.at[g, o],
            device_id={"col": lax.rem(me + o, n_col)}, device_id_type=MESH)

    def back(g, o, landing):
        start, size = groups[g]
        part = pl.ds(start * SUB // 2, size * SUB // 2)
        return pltpu.make_async_remote_copy(
            src_ref=ysend.at[lax.rem(me + o, n_col), part], dst_ref=yrecv.at[landing, part],
            send_sem=ys_sem.at[g, o], recv_sem=yr_sem.at[g, o],
            device_id={"col": lax.rem(me + o, n_col)}, device_id_type=MESH)

    for g in range(len(groups)):
        for o in range(1, n_col):
            forth(g, o, me).start()
    own = pltpu.make_async_copy(send.at[me], recv.at[me], l_sem.at[0])
    own.start()

    w2.wait()
    for t in range(inner // LANES):
        z = jnp.dot(x, win[:, inner + t * LANES:inner + (t + 1) * LANES], preferred_element_type=f32)
        z = z.astype(bf16).astype(f32)
        zs[:, t * LANES:(t + 1) * LANES] = z * jax.nn.sigmoid(z)
    state[...] = jnp.zeros_like(state)
    own.wait()

    rate_x, rate_y, skip = ratex_ref[head], ratey_ref[head], skip_ref[head]
    down = lax.broadcasted_iota(jnp.int32, (jp, jp), 0)
    along = lax.broadcasted_iota(jnp.int32, (jp, jp), 1)
    tri = (along <= down).astype(bf16)
    cell_lane = lax.broadcasted_iota(jnp.int32, (jp, LANES), 1)

    def scan_rows(m, total):
        decays = []
        for k in range(2):
            both = recv[:, pl.ds(pl.multiple_of(m * 32 + k * 16, 16), 16), :].astype(f32)
            for p in range(2):
                i = 4 * m + 2 * k + p
                here = both[:, p * SUB:(p + 1) * SUB, :].reshape(jp, LANES)
                sums = jnp.dot(tri, here.astype(bf16), preferred_element_type=f32)
                sum_col = sums[:, dt_at:dt_at + 1]
                turned = jnp.where(cell_lane == dt_at + 1, sum_col, here).T
                tsc[i] = turned
                gap = turned[dt_at + 1:dt_at + 2, :] - sum_col
                decays.append(jnp.exp(jnp.where(down <= along, -rate_x * gap, -1e30)).astype(bf16))
                total = total + turned[dt_at:dt_at + 1, :]
                fade[i] = turned[ch + n_state:dt_at, :] * jnp.exp(-rate_y * total)
        for cb in range(blocks):
            now = state[cb]
            for r in range(4):
                i = 4 * m + r
                v = tsc[i, cb * block:(cb + 1) * block, :]
                b = tsc[i, ch:ch + n_state, :]
                c = tsc[i, ch + n_state:ch + 2 * n_state, :]
                dt = tsc[i, dt_at:dt_at + 1, :]
                source = (b[:, None, :] * (v * dt)[None, :, :]).reshape(n_state * block, jp)
                hx = jnp.dot(source.astype(bf16), decays[r], preferred_element_type=f32)
                now = jnp.exp(-rate_y * dt) * now + hx
                y = jnp.sum(c[:, None, :] * now.reshape(n_state, block, jp), axis=0) + skip * v
                ysc[i, cb * block:(cb + 1) * block, :] = y
            state[cb] = now
        return total

    def give_back(m, _):
        parts = []
        for k in range(2):
            pair = [ysc[4 * m + 2 * k], ysc[4 * m + 2 * k + 1]]
            if 2 * ch < LANES:
                pair.append(jnp.zeros((LANES - 2 * ch, jp), f32))
            parts.append(jnp.concatenate(pair, axis=0).T.reshape(n_col, SUB, LANES))
        ysend[:, pl.ds(pl.multiple_of(m * 16, 16), 16), :] = jnp.concatenate(parts, axis=1).astype(bf16)
        return 0

    def return_group(g):
        start, size = groups[g]
        lax.fori_loop(start // 4, (start + size) // 4, give_back, 0)
        for o in range(1, n_col):
            back(g, o, me).start()

    total = jnp.zeros((1, jp), f32)
    for g in range(len(groups)):
        start, size = groups[g]
        for o in range(1, n_col):
            forth(g, o, lax.rem(me + n_col - o, n_col)).wait_recv()
        total = lax.fori_loop(start // 4, (start + size) // 4, scan_rows, total)

        @pl.when(my_row == 0)
        def _():
            return_group(g)

    def pass_down(cb, to):
        return pltpu.make_async_remote_copy(
            src_ref=state.at[cb], dst_ref=carry.at[cb],
            send_sem=cs_sem.at[cb], recv_sem=cr_sem.at[cb],
            device_id={"row": to}, device_id_type=MESH)

    @pl.when(my_row == 0)
    def _():
        for cb in range(blocks):
            pass_down(cb, my_row + 1).start()

    @pl.when(my_row > 0)
    def _():
        for cb in range(blocks):
            pass_down(cb, my_row - 1).wait_recv()
            if n_row > 2:
                @pl.when(my_row < n_row - 1)
                def _():
                    state[cb] = state[cb] + jnp.exp(-rate_y * total) * carry[cb]
                    pass_down(cb, my_row + 1).start()

        def correct(m, _):
            for cb in range(blocks):
                held = carry[cb].reshape(n_state, block, jp)
                for r in range(4):
                    i = 4 * m + r
                    more = jnp.sum(fade[i][:, None, :] * held, axis=0)
                    ysc[i, cb * block:(cb + 1) * block, :] = ysc[i, cb * block:(cb + 1) * block, :] + more
            return 0

        for g in range(len(groups)):
            start, size = groups[g]
            lax.fori_loop(start // 4, (start + size) // 4, correct, 0)
            return_group(g)

    own_y = pltpu.make_async_copy(ysend.at[me], yrecv.at[me], l_sem.at[1])
    own_y.start()
    w3.wait()
    own_y.wait()

    @pl.when(my_row < n_row - 1)
    def _():
        for cb in range(blocks):
            pass_down(cb, my_row + 1).wait_send()

    for g in range(len(groups)):
        for o in range(1, n_col):
            forth(g, o, me).wait_send()
            back(g, o, lax.rem(me + n_col - o, n_col)).wait()

    half_lane = lax.broadcasted_iota(jnp.int32, (cells // 2, LANES), 1)
    squares = jnp.zeros((cells, 1), f32)
    for t in range(inner // LANES):
        parts = []
        for p in range(2):
            tile = None
            for q in range(per):
                piece = yrecv[t * per + q].astype(f32)
                shift = ((q - p) * ch) % LANES
                if shift:
                    piece = pltpu.roll(piece, shift, 1)
                tile = piece if tile is None else jnp.where(half_lane < q * ch, tile, piece)
            parts.append(tile.reshape(rows // 2, 1, SUB, LANES))
        y = jnp.concatenate(parts, axis=1).reshape(cells, LANES)
        z = zs[:, t * LANES:(t + 1) * LANES]
        g = y * z
        squares = squares + jnp.sum(g * g, axis=1, keepdims=True)
        yfull[:, t * LANES:(t + 1) * LANES] = g
    scale = lax.rsqrt(squares / inner + norm_eps)
    normed = (yfull[...] * scale * gain_ref[...]).astype(bf16)
    mixed = jnp.dot(normed, wout[...], preferred_element_type=f32) * mask
    out_ref[...] = mixed.reshape(rows, SUB, mixed.shape[1])[:, :cols, :].astype(bf16)


def per_device(slide, tissue, w_in, w_bcd, dt_bias, rate_x, rate_y, d_skip, norm_gain, w_out):
    rows, cols, model = slide.shape
    inner, heads = w_out.shape[0], dt_bias.shape[0]
    n_state = (w_bcd.shape[1] - heads) // 2
    width = inner // heads
    n_col, n_row = lax.axis_size("col"), lax.axis_size("row")
    ch = inner // n_col
    block = min(ch, 16)
    jp, cells = n_col * SUB, rows * SUB
    assert cols <= SUB and n_row > 1 and rows <= LANES and rows % 4 == 0 and 2 * ch <= LANES and width % ch == 0
    assert ch + 2 * n_state + heads <= LANES and ch % block == 0
    units = rows // 4
    splits = min(4, units)
    edges = [4 * ((units * g + splits - 1) // splits) for g in range(splits + 1)]
    groups = tuple((lo, hi - lo) for lo, hi in zip(edges[:-1], edges[1:]))
    vmem = pl.BlockSpec(memory_space=pltpu.VMEM)
    smem = pl.BlockSpec(memory_space=pltpu.SMEM)
    hbm = pl.BlockSpec(memory_space=pl.ANY)
    blocks = ch // block
    dims = (n_row, n_col, rows, cols, inner, heads, width, n_state, block, groups)
    dma = pltpu.SemaphoreType.DMA
    return pl.pallas_call(
        functools.partial(kernel, dims),
        out_shape=jax.ShapeDtypeStruct((rows, cols, model), bf16),
        in_specs=[vmem] * 4 + [smem] * 4 + [hbm] * 2,
        out_specs=vmem,
        scratch_shapes=[
            pltpu.VMEM(w_in.shape, bf16),
            pltpu.VMEM(w_out.shape, bf16),
            pltpu.VMEM((n_col, cells, LANES), bf16),
            pltpu.VMEM((n_col, cells, LANES), bf16),
            pltpu.VMEM((cells, inner), f32),
            pltpu.VMEM((rows, LANES, jp), f32),
            pltpu.VMEM((rows, n_state, jp), f32),
            pltpu.VMEM((rows, ch, jp), f32),
            pltpu.VMEM((blocks, n_state * block, jp), f32),
            pltpu.VMEM((blocks, n_state * block, jp), f32),
            pltpu.VMEM((n_col, cells // 2, LANES), bf16),
            pltpu.VMEM((n_col, cells // 2, LANES), bf16),
            pltpu.VMEM((cells, inner), f32),
            dma((3,)), *[dma((splits, n_col))] * 4,
            dma((blocks,)), dma((blocks,)), dma((2,)),
        ],
        compiler_params=pltpu.CompilerParams(
            collective_id=0, has_side_effects=True, vmem_limit_bytes=60 * 1024 * 1024),
        cost_estimate=pl.CostEstimate(flops=4 * 10**9, bytes_accessed=8 * 10**6, transcendentals=10**6),
    )(slide, tissue.T, w_bcd.T, norm_gain.reshape(1, inner), dt_bias, rate_x, rate_y, d_skip, w_in, w_out)


def solution(mesh):
    grid = P(("slides", "row"), "col")
    return jax.shard_map(
        per_device,
        mesh=mesh,
        in_specs=(P(("slides", "row"), "col", None), grid) + (P(),) * 8,
        out_specs=P(("slides", "row"), "col", None),
        check_vma=False,
    )
```

time: 74.5 us -> 49.7 us (0.67)
  Pallas kernels: 65.8 us -> 47.7 us
  local copies, waits for them, and re-layouts: 7.74 us -> 1.82 us
    pallas_call x1, Pallas kernels: 65.8 us -> 47.7 us  [per_device(): pl.pallas_call(functools.partial(kernel, dims), out_shape=jax.ShapeDtypeS...]
    reshape x3 -> x0, local copies, waits for them, and re-layouts: 3.91 us -> none  [the longest x1 1.88 us: per_device(): x = jnp.pad(slide, ((0, 0), (0, pad), (0, 0))).reshape(cells, model)]
    unnamed x3 -> x1, local copies, waits for them, and re-layouts: 2.98 us -> 1.82 us
    pad x2 -> x0, local copies, waits for them, and re-layouts: 0.85 us -> none  [the longest x1 0.84 us: per_device(): wbcd = jnp.pad(w_bcd, ((0, 0), (ch, room)))]
where the time goes in v2:
time: 49.7 us; the launch traced here: 49.5 us
  Pallas kernels  47.7 us (96%)
  local copies, waits for them, and re-layouts  1.82 us (4%)
    pallas_call x1, Pallas kernels, per_device(): pl.pallas_call(functools.partial(kernel, dims), out_shape=jax.ShapeDtypeS...  47.7 us
    unnamed x1, local copies, waits for them, and re-layouts  1.82 us

profile of v2, /device:TPU:1, one launch (start us, length us, event | category | flops | bytes accessed | tf_op | source)
XLA Modules:
  0.0 49.5 jit_solution(10861654937258872277)
XLA Ops:
  0.0 47.7 %shard_map.100 = bf16[28,7,1024]{2,1,0:T(8,128)(2,1)} custom-call(bf16[28,7,1024]{2,1,0:T(8,128)(2,1)} %slide_ref.1, s32[7,28]{1,0:T(8,128)} %bitcast.4, bf16[48,1024]{1,0:T(8,128)(2,1)} %bitcast.3, f32[1,1024]{1,0:T(1,128)} %bitcast.5, f32[16]{0:T(128)} %bias_ref.1, f32[16]{0:T(128)} %ratex_ref.1, f32[16]{0:T(128)} %ratey_ref.1, f32[16]{0:T(128)} %skip_ref.1, ...), custom_call_target="tpu_custom_call" | custom-call | flops 4000000000 | bytes 8000000 | tf_op jit(solution)/shard_map/pallas_call | solution.py:273
  47.7 1.8 %copy.12 = bf16[28,7,1024]{2,1,0:T(8,128)(2,1)} copy(bf16[28,7,1024]{2,1,0:T(8,128)(2,1)} %shard_map.100) | data formatting | bytes 802816
